TPU v7x, 1024 devices: a whole 4x4x32 slice. The times are simulated.
1024 devices in a mesh: pipe: 16 (over x, y_lo, core), expert: 64 (over z, y_hi).
Axes of the slice: x: 4, y: 4 (y_hi: 2, y_lo: 2; y = y_hi * 2 + y_lo), z: 32, core: 2. Of those that a mesh axis runs over, the one named last changes fastest.
Arguments:
- fwd_tokens: bfloat16 [16, 512, 7168], P('pipe', 'expert'), may hold values from -6 to 6
- fwd_routes: int32 [16, 512, 1], P('pipe', 'expert'), may hold values from 0 to 3, as said below
- fwd_weight: float32 [16, 512, 1], P('pipe', 'expert'), may hold values from 0.2 to 1
- bwd_grad: bfloat16 [16, 512, 7168], P('pipe', 'expert'), may hold values from -6 to 6
- bwd_routes: int32 [16, 512, 1], P('pipe', 'expert'), may hold values from 0 to 3, as said below
- bwd_weight: float32 [16, 512, 1], P('pipe', 'expert'), may hold values from 0.2 to 1
- gate_saved: float32 [16, 256, 4096], P('pipe', None, 'expert'), may hold values from -6 to 6
- up_saved: float32 [16, 256, 4096], P('pipe', None, 'expert'), may hold values from -6 to 6
- gate_proj: bfloat16 [16, 64, 3584, 128], P('pipe', 'expert'), may hold values from -0.0625 to 0.0625
- up_proj: bfloat16 [16, 64, 3584, 128], P('pipe', 'expert'), may hold values from -0.0625 to 0.0625
- down_proj: bfloat16 [16, 64, 128, 3584], P('pipe', 'expert'), may hold values from -0.1875 to 0.1875
Outputs:
- fwd_next: bfloat16 [16, 512, 7168], P('pipe', 'expert')
- bwd_next: bfloat16 [16, 512, 7168], P('pipe', 'expert')
Inputs may be any that keep to these rules, and one draw needn't show every extreme that they name: `fwd_routes`: each token names one expert of the window. Among the 8 tokens of one device no expert is named by more than 4 routes, and in each section one expert is named by exactly 4 routes of every device. `bwd_routes`: as fwd_routes.
All inputs are finite; a program needn't handle non-finite values.
Results may differ from a plain program's by a relative error of at most 0.013.
Values may be sent and summed in bfloat16 or wider, within the bound.
A program may use at most 64 MiB of HBM per device.

v0:
```python
import jax
import jax.numpy as jnp
from jax import lax
from jax.sharding import PartitionSpec as P


def swapped(value, axis, apart):
    mask = 2**apart
    pairs = [(source, source ^ mask) for source in range(lax.axis_size(axis))]
    return lax.ppermute(value, axis, pairs)


def from_behind(value, axis, steps):
    count = lax.axis_size(axis)
    pairs = [(source, (source + steps) % count) for source in range(count)]
    return lax.ppermute(value, axis, pairs)


def build_sel(routes_dev, experts, capacity):
    flat = routes_dev.reshape(-1)
    onehot = (flat[:, None] == jnp.arange(experts, dtype=jnp.int32)[None, :]).astype(jnp.int32)
    before = jnp.cumsum(onehot, axis=0) - onehot
    position = jnp.sum(before * onehot, axis=1)
    place = flat * capacity + position
    return (jnp.arange(experts * capacity, dtype=jnp.int32)[:, None] == place[None, :]).astype(
        jnp.bfloat16
    )


def spread(block, experts, capacity, splits, piece_width, shards):
    pieces = block.reshape(experts, 1, capacity, splits, piece_width)
    pieces = jnp.broadcast_to(pieces, (experts, shards, capacity, splits, piece_width))
    return jnp.transpose(pieces, (0, 1, 3, 2, 4)).reshape(
        experts * shards * splits, capacity, piece_width
    )


def add_halves(values):
    values = values + swapped(values.astype(jnp.bfloat16), "expert", 0).astype(values.dtype)
    return values


def sum_shards(received, experts, capacity, splits, piece_width, shards):
    summed = jnp.sum(
        received.reshape(experts, shards, splits, capacity, piece_width).astype(jnp.float32), axis=1
    )
    return (
        jnp.transpose(summed, (0, 2, 1, 3))
        .reshape(experts * capacity, splits * piece_width)
        .astype(jnp.bfloat16)
    )


def contract_rows(left, right):
    return lax.dot_general(
        left, right, (((0,), (0,)), ((), ())), preferred_element_type=jnp.float32
    )


def contract_cols(left, right):
    return lax.dot_general(
        left, right, (((1,), (1,)), ((), ())), preferred_element_type=jnp.float32
    )


def per_device(
    fwd_tokens,
    fwd_routes,
    fwd_weight,
    bwd_grad,
    bwd_routes,
    bwd_weight,
    gate_saved,
    up_saved,
    gate_proj,
    up_proj,
    down_proj,
):
    devices = lax.axis_size("expert")
    group_size = min(16, devices // 2)
    shards = min(8, group_size)
    splits = group_size // shards
    experts = devices // group_size
    slot_rows = gate_saved.shape[1]
    capacity = slot_rows // devices
    width = fwd_tokens.shape[2]
    piece_width = width // splits
    routes = fwd_routes.shape[2]
    own_index = lax.axis_index("expert")
    w_gate = gate_proj[0, 0]
    w_up = up_proj[0, 0]
    w_down = down_proj[0, 0]
    shard_width = w_gate.shape[1]
    tokens = fwd_tokens[0]
    grads = bwd_grad[0]
    select_fwd = build_sel(fwd_routes[0], experts, capacity)
    select_bwd = build_sel(bwd_routes[0], experts, capacity)
    token_rows = jnp.repeat(tokens, routes, axis=0)
    scaled = (bwd_weight[0] * jnp.repeat(grads, routes, axis=0).astype(jnp.float32)).astype(
        jnp.bfloat16
    )
    send_fwd = jnp.dot(select_fwd, token_rows, preferred_element_type=jnp.float32).astype(
        jnp.bfloat16
    )
    send_bwd = jnp.dot(select_bwd, scaled, preferred_element_type=jnp.float32).astype(jnp.bfloat16)
    got_fwd, got_bwd = (
        lax.all_to_all(
            spread(send_fwd, experts, capacity, splits, piece_width, shards),
            "expert",
            split_axis=0,
            concat_axis=0,
            tiled=True,
        ),
        lax.all_to_all(
            spread(send_bwd, experts, capacity, splits, piece_width, shards),
            "expert",
            split_axis=0,
            concat_axis=0,
            tiled=True,
        ),
    )
    rows_fwd = got_fwd.reshape(slot_rows, piece_width)
    rows_bwd = got_bwd.reshape(slot_rows, piece_width)
    pre_sums = jnp.concatenate(
        [
            jnp.dot(rows_fwd, w_gate, preferred_element_type=jnp.float32),
            jnp.dot(rows_fwd, w_up, preferred_element_type=jnp.float32),
        ],
        axis=1,
    )
    pre_sums = add_halves(pre_sums)
    hidden = (jax.nn.silu(pre_sums[:, :shard_width]) * pre_sums[:, shard_width:]).astype(
        jnp.bfloat16
    )
    out_fwd = jnp.dot(hidden, w_down, preferred_element_type=jnp.float32).astype(jnp.bfloat16)
    down_part = contract_cols(rows_bwd, w_down)
    placer = (jnp.arange(splits, dtype=jnp.int32) == own_index % splits).astype(jnp.float32)
    gate_full = (placer[None, :, None] * gate_saved[0][:, None, :]).reshape(slot_rows, shard_width)
    up_full = (placer[None, :, None] * up_saved[0][:, None, :]).reshape(slot_rows, shard_width)
    joined = add_halves(jnp.concatenate([down_part, gate_full, up_full], axis=1))
    hidden_grad = joined[:, :shard_width]
    gate_pre = joined[:, shard_width : 2 * shard_width]
    up_pre = joined[:, 2 * shard_width :]
    logistic = jax.nn.sigmoid(gate_pre)
    gate_grad = (hidden_grad * up_pre * logistic * (1.0 + gate_pre * (1.0 - logistic))).astype(
        jnp.bfloat16
    )
    up_grad = (hidden_grad * gate_pre * logistic).astype(jnp.bfloat16)
    out_bwd = (contract_cols(gate_grad, w_gate) + contract_cols(up_grad, w_up)).astype(jnp.bfloat16)
    back_fwd, back_bwd = (
        lax.all_to_all(
            out_fwd.reshape(devices, capacity, piece_width),
            "expert",
            split_axis=0,
            concat_axis=0,
            tiled=True,
        ),
        lax.all_to_all(
            out_bwd.reshape(devices, capacity, piece_width),
            "expert",
            split_axis=0,
            concat_axis=0,
            tiled=True,
        ),
    )
    expert_fwd = sum_shards(back_fwd, experts, capacity, splits, piece_width, shards)
    expert_bwd = sum_shards(back_bwd, experts, capacity, splits, piece_width, shards)
    routed_fwd = contract_rows(select_fwd, expert_fwd).reshape(-1, routes, width)
    mixed = (
        tokens.astype(jnp.float32) + jnp.sum(fwd_weight[0][:, :, None] * routed_fwd, axis=1)
    ).astype(jnp.bfloat16)
    routed_bwd = contract_rows(select_bwd, expert_bwd).reshape(-1, routes, width)
    grad_in = (grads.astype(jnp.float32) + jnp.sum(routed_bwd, axis=1)).astype(jnp.bfloat16)
    sent_fwd, sent_bwd = from_behind((mixed, grad_in), "pipe", 1)
    return (sent_fwd[None], sent_bwd[None])


def solution(mesh):
    in_specs = (
        P("pipe", "expert", None),
        P("pipe", "expert", None),
        P("pipe", "expert", None),
        P("pipe", "expert", None),
        P("pipe", "expert", None),
        P("pipe", "expert", None),
        P("pipe", None, "expert"),
        P("pipe", None, "expert"),
        P("pipe", "expert", None, None),
        P("pipe", "expert", None, None),
        P("pipe", "expert", None, None),
    )
    out_specs = (P("pipe", "expert", None), P("pipe", "expert", None))
    return jax.shard_map(
        per_device, mesh=mesh, in_specs=in_specs, out_specs=out_specs, check_vma=False
    )
```

profile of v0, /device:TPU:1, one launch (start us, length us, event | category | flops | bytes accessed | tf_op | source)
XLA Modules:
  0.0 775.4 jit_solution(9413860047299123062)
XLA Ops:
  0.6 0.7 fusion.35
  1.6 0.7 select_reduce_fusion.1
  2.9 1.1 convolution_convert_fusion.1
  4.3 1.8 broadcast_in_dim.13
  6.0 32.7 %all-to-all-start = ((bf16[64,4,3584]{2,1,0:T(4,128)(2,1)}), bf16[64,4,3584]{2,1,0:T(4,128)(2,1)S(1)}, u32[]{:S(2)}, u32[]{:S(2)}) async-start(bf16[64,4,3584]{2,1,0:T(4,128)(2,1)} %bitcast.63), calls=%async_computation | async-start | bytes 3670016 | tf_op jit(solution)/shard_map/all_to_all | solution.py:107
  39.5 167.8 %all-to-all-done = bf16[64,4,3584]{2,1,0:T(4,128)(2,1)S(1)} async-done(((bf16[64,4,3584]{2,1,0:T(4,128)(2,1)}), bf16[64,4,3584]{2,1,0:T(4,128)(2,1)S(1)}, u32[]{:S(2)}, u32[]{:S(2)}) %all-to-all-start) | async-done | bytes 1835040 | tf_op jit(solution)/shard_map/all_to_all | solution.py:107
  207.3 1.8 broadcast_in_dim.32
  209.2 14.4 %all-to-all-start.2 = ((bf16[64,4,3584]{2,1,0:T(4,128)(2,1)}), bf16[64,4,3584]{2,1,0:T(4,128)(2,1)}, u32[]{:S(2)}, u32[]{:S(2)}) async-start(bf16[64,4,3584]{2,1,0:T(4,128)(2,1)} %bitcast.62), calls=%async_computation.2 | async-start | bytes 3670016 | tf_op jit(solution)/shard_map/all_to_all | solution.py:114
  223.5 2.9 reshape.81
  226.5 2.0 fusion.12
  228.5 0.8 fusion.8
  229.3 4.4 collective-permute-start
  233.7 3.3 collective-permute-done
  237.0 0.7 convolution_convert_fusion.2
  237.7 1.5 reshape.82
  239.2 152.7 %all-to-all-done.2 = bf16[64,4,3584]{2,1,0:T(4,128)(2,1)} async-done(((bf16[64,4,3584]{2,1,0:T(4,128)(2,1)}), bf16[64,4,3584]{2,1,0:T(4,128)(2,1)}, u32[]{:S(2)}, u32[]{:S(2)}) %all-to-all-start.2) | async-done | bytes 1835040 | tf_op jit(solution)/shard_map/all_to_all | solution.py:114
  391.9 14.3 %all-to-all-start.1 = ((bf16[64,4,3584]{2,1,0:T(4,128)(2,1)}), bf16[64,4,3584]{2,1,0:T(4,128)(2,1)S(1)}, u32[]{:S(2)}, u32[]{:S(2)}) async-start(bf16[64,4,3584]{2,1,0:T(4,128)(2,1)} %reshape.82), calls=%async_computation.1 | async-start | bytes 3670016 | tf_op jit(solution)/shard_map/all_to_all | solution.py:151
  406.5 3.9 reshape.84
  410.4 2.3 fusion.4
  412.7 4.4 collective-permute-start.2
  417.1 4.9 collective-permute-done.2
  422.1 0.7 fusion.10
  423.3 1.9 fusion.3
  425.2 4.1 reshape.85
  429.3 145.4 %all-to-all-done.1 = bf16[64,4,3584]{2,1,0:T(4,128)(2,1)S(1)} async-done(((bf16[64,4,3584]{2,1,0:T(4,128)(2,1)}), bf16[64,4,3584]{2,1,0:T(4,128)(2,1)S(1)}, u32[]{:S(2)}, u32[]{:S(2)}) %all-to-all-start.1) | async-done | bytes 1835040 | tf_op jit(solution)/shard_map/all_to_all | solution.py:151
  574.7 14.7 %all-to-all-start.3 = ((bf16[64,4,3584]{2,1,0:T(4,128)(2,1)}), bf16[64,4,3584]{2,1,0:T(4,128)(2,1)}, u32[]{:S(2)}, u32[]{:S(2)}) async-start(bf16[64,4,3584]{2,1,0:T(4,128)(2,1)} %reshape.85), calls=%async_computation.3 | async-start | bytes 3670016 | tf_op jit(solution)/shard_map/all_to_all | solution.py:158
  589.4 1.0 reduce
  590.9 3.0 collective-permute-start.1
  593.9 163.8 %all-to-all-done.3 = bf16[64,4,3584]{2,1,0:T(4,128)(2,1)} async-done(((bf16[64,4,3584]{2,1,0:T(4,128)(2,1)}), bf16[64,4,3584]{2,1,0:T(4,128)(2,1)}, u32[]{:S(2)}, u32[]{:S(2)}) %all-to-all-start.3) | async-done | bytes 1835040 | tf_op jit(solution)/shard_map/all_to_all | solution.py:158
  757.7 2.4 reduce.1
  760.5 11.8 %collective-permute-start.3 = (bf16[8,7168]{1,0:T(8,128)(2,1)S(1)}, bf16[8,7168]{1,0:T(8,128)(2,1)S(1)}, u32[]{:S(2)}, u32[]{:S(2)}) collective-permute-start(bf16[8,7168]{1,0:T(8,128)(2,1)S(1)} %fusion.2), channel_id=1, source_target_pairs={{0,64},{64,128},{128,192},{192,256},{256,320},{320,384},{384,448},... | collective-permute-start | bytes 344072 | tf_op jit(solution)/shard_map/ppermute | solution.py:16
  772.3 1.8 collective-permute-done.3
  (52 shorter events, 4.8 us)
Async XLA Ops:
  0.6 236.4 %copy-start = (bf16[1,1,128,3584]{3,2,1,0:T(8,128)(2,1)S(1)}, bf16[1,1,128,3584]{3,2,1,0:T(8,128)(2,1)}, u32[]{:S(2)}) copy-start(bf16[1,1,128,3584]{3,2,1,0:T(8,128)(2,1)} %param.21) | copy-start | bytes 2752516
  6.0 32.7 %copy-start.9 = (s32[1,8,1]{1,2,0:T(1,128)S(1)}, s32[1,8,1]{1,2,0:T(1,128)}, u32[]{:S(2)}) copy-start(s32[1,8,1]{1,2,0:T(1,128)} %param.15) | copy-start | bytes 100
  6.0 32.9 %copy-start.6 = (bf16[1,8,7168]{2,1,0:T(8,128)(2,1)S(1)}, bf16[1,8,7168]{2,1,0:T(8,128)(2,1)}, u32[]{:S(2)}) copy-start(bf16[1,8,7168]{2,1,0:T(8,128)(2,1)} %param.14) | copy-start | bytes 344068
  6.0 32.9 %copy-start.10 = (f32[1,8,1]{1,2,0:T(1,128)S(1)}, f32[1,8,1]{1,2,0:T(1,128)}, u32[]{:S(2)}) copy-start(f32[1,8,1]{1,2,0:T(1,128)} %param.16) | copy-start | bytes 100
  6.0 201.3 %all-to-all-start = ((bf16[64,4,3584]{2,1,0:T(4,128)(2,1)}), bf16[64,4,3584]{2,1,0:T(4,128)(2,1)S(1)}, u32[]{:S(2)}, u32[]{:S(2)}) async-start(bf16[64,4,3584]{2,1,0:T(4,128)(2,1)} %bitcast.63), calls=%async_computation | async-start | bytes 3670016 | tf_op jit(solution)/shard_map/all_to_all | solution.py:107
  207.3 1.8 copy-start.1
  209.2 182.7 %all-to-all-start.2 = ((bf16[64,4,3584]{2,1,0:T(4,128)(2,1)}), bf16[64,4,3584]{2,1,0:T(4,128)(2,1)}, u32[]{:S(2)}, u32[]{:S(2)}) async-start(bf16[64,4,3584]{2,1,0:T(4,128)(2,1)} %bitcast.62), calls=%async_computation.2 | async-start | bytes 3670016 | tf_op jit(solution)/shard_map/all_to_all | solution.py:114
  226.5 2.0 copy-start.3
  229.3 7.6 collective-permute-start
  239.2 167.2 %copy-start.7 = (f32[1,256,64]{1,2,0:T(8,128)S(1)}, f32[1,256,64]{1,2,0:T(8,128)}, u32[]{:S(2)}) copy-start(f32[1,256,64]{1,2,0:T(8,128)} %param.17) | copy-start | bytes 196612
  239.2 167.2 %copy-start.8 = (f32[1,256,64]{1,2,0:T(8,128)S(1)}, f32[1,256,64]{1,2,0:T(8,128)}, u32[]{:S(2)}) copy-start(f32[1,256,64]{1,2,0:T(8,128)} %param.18) | copy-start | bytes 196612
  391.9 182.7 %all-to-all-start.1 = ((bf16[64,4,3584]{2,1,0:T(4,128)(2,1)}), bf16[64,4,3584]{2,1,0:T(4,128)(2,1)S(1)}, u32[]{:S(2)}, u32[]{:S(2)}) async-start(bf16[64,4,3584]{2,1,0:T(4,128)(2,1)} %reshape.82), calls=%async_computation.1 | async-start | bytes 3670016 | tf_op jit(solution)/shard_map/all_to_all | solution.py:151
  410.4 11.7 %copy-start.2 = (bf16[1,1,3584,128]{3,2,1,0:T(8,128)(2,1)S(1)}, bf16[1,1,3584,128]{3,2,1,0:T(8,128)(2,1)}, u32[]{:S(2)}) copy-start(bf16[1,1,3584,128]{3,2,1,0:T(8,128)(2,1)} %param.19) | copy-start | bytes 2752516
  412.7 9.3 %collective-permute-start.2 = (bf16[256,384]{0,1:T(8,128)(2,1)S(1)}, bf16[256,384]{0,1:T(8,128)(2,1)S(1)}, u32[]{:S(2)}, u32[]{:S(2)}) collective-permute-start(bf16[256,384]{0,1:T(8,128)(2,1)S(1)} %fusion.14), channel_id=1, source_target_pairs={{0,1},{1,0},{2,3},{3,2},{4,5},{5,4},{6,7},{7,6},{8,9},{9,8},{10,11... | collective-permute-start | bytes 589832 | tf_op jit(solution)/shard_map/ppermute | solution.py:10
  422.1 1.2 copy-start.4
  574.7 183.0 %all-to-all-start.3 = ((bf16[64,4,3584]{2,1,0:T(4,128)(2,1)}), bf16[64,4,3584]{2,1,0:T(4,128)(2,1)}, u32[]{:S(2)}, u32[]{:S(2)}) async-start(bf16[64,4,3584]{2,1,0:T(4,128)(2,1)} %reshape.85), calls=%async_computation.3 | async-start | bytes 3670016 | tf_op jit(solution)/shard_map/all_to_all | solution.py:158
  589.4 1.3 copy-start.5
  589.4 1.3 copy-start.11
  590.9 181.4 %collective-permute-start.1 = (bf16[8,7168]{1,0:T(8,128)(2,1)S(1)}, bf16[8,7168]{1,0:T(8,128)(2,1)S(1)}, u32[]{:S(2)}, u32[]{:S(2)}) collective-permute-start(bf16[8,7168]{1,0:T(8,128)(2,1)S(1)} %fusion.1), channel_id=1, source_target_pairs={{0,64},{64,128},{128,192},{192,256},{256,320},{320,384},{384,448},... | collective-permute-start | bytes 344072 | tf_op jit(solution)/shard_map/ppermute | solution.py:16
  760.5 13.6 %collective-permute-start.3 = (bf16[8,7168]{1,0:T(8,128)(2,1)S(1)}, bf16[8,7168]{1,0:T(8,128)(2,1)S(1)}, u32[]{:S(2)}, u32[]{:S(2)}) collective-permute-start(bf16[8,7168]{1,0:T(8,128)(2,1)S(1)} %fusion.2), channel_id=1, source_target_pairs={{0,64},{64,128},{128,192},{192,256},{256,320},{320,384},{384,448},... | collective-permute-start | bytes 344072 | tf_op jit(solution)/shard_map/ppermute | solution.py:16
where the time goes:
time: 779 us; the launch traced here: 775 us
  waiting for transfers between devices  640 us (82%)
  starting transfers between devices  99.5 us (13%)
  local copies, waits for them, and re-layouts  18.9 us (2%)
  matrix products  10.2 us (1%)
    all_to_all x1, waiting for transfers between devices, per_device(): lax.all_to_all(spread(send_fwd, experts, capacity, splits, piece_width, s...  168 us
    all_to_all x1, waiting for transfers between devices, per_device(): lax.all_to_all(out_bwd.reshape(devices, capacity, piece_width), 'expert',...  164 us
    all_to_all x1, waiting for transfers between devices, per_device(): lax.all_to_all(spread(send_bwd, experts, capacity, splits, piece_width, s...  153 us
    all_to_all x1, waiting for transfers between devices, per_device(): lax.all_to_all(out_fwd.reshape(devices, capacity, piece_width), 'expert',...  145 us
    all_to_all x1, starting transfers between devices, per_device(): lax.all_to_all(spread(send_fwd, experts, capacity, splits, piece_width, s...  32.7 us
  transfers between devices with their start and end apart: 8, of which 7 were waited for; matrix products, arithmetic and copies ran while one was open for 3% of the time, Pallas kernels for 0%

commit v1 on v0

v1 whole, which is shorter than its diff:
```python
import jax
import jax.numpy as jnp
from jax import lax
from jax.sharding import PartitionSpec as P


def pair_swap(value):
    count = lax.axis_size("expert")
    return lax.ppermute(value, "expert", [(s, s ^ 1) for s in range(count)])


def from_behind(value, axis, steps):
    count = lax.axis_size(axis)
    return lax.ppermute(value, axis, [(s, (s + steps) % count) for s in range(count)])


def columns():
    count = lax.axis_size("expert")
    return [list(range(0, count, 2)), list(range(1, count, 2))]


def halves(rows, own_i):
    half = rows.shape[1] // 2
    first, second = rows[:, :half], rows[:, half:]
    keep = jnp.where(own_i == 0, first, second)
    send = jnp.where(own_i == 0, second, first)
    got = pair_swap(send)
    return jnp.where(own_i == 0, jnp.concatenate([keep, got]), jnp.concatenate([got, keep]))


def rejoin(rows, own_i):
    tok = rows.shape[0] // 2
    keep = jnp.where(own_i == 0, rows[:tok], rows[tok:])
    send = jnp.where(own_i == 0, rows[tok:], rows[:tok])
    got = pair_swap(send)
    return jnp.where(
        own_i == 0,
        jnp.concatenate([keep, got], axis=1),
        jnp.concatenate([got, keep], axis=1),
    )


def contract_cols(left, right):
    return lax.dot_general(
        left, right, (((1,), (1,)), ((), ())), preferred_element_type=jnp.float32
    )


def contract_rows(left, right):
    return lax.dot_general(
        left, right, (((0,), (0,)), ((), ())), preferred_element_type=jnp.float32
    )


def place_of(routes, own_g, tok, cap):
    mine = (routes.reshape(-1, tok) == own_g).astype(jnp.int32)
    before = jnp.cumsum(mine, axis=1) - mine
    slot = jnp.arange(mine.shape[0], dtype=jnp.int32)[:, None] * cap + before
    return jnp.where(mine == 1, slot, -1).reshape(-1)


def per_device(tokens, routes_f, weight_f, grads, routes_b, weight_b, gate_saved, up_saved,
               gate_proj, up_proj, down_proj):
    tokens, grads = tokens[0], grads[0]
    w_gate, w_up, w_down = gate_proj[0, 0], up_proj[0, 0], down_proj[0, 0]
    devices = lax.axis_size("expert")
    tok = tokens.shape[0]
    slots = gate_saved.shape[1]
    cap = slots // devices
    own = lax.axis_index("expert")
    own_i = own % 2
    own_g = own // 16
    scaled = (weight_b[0] * grads.astype(jnp.float32)).astype(jnp.bfloat16)
    routes = jnp.concatenate([routes_f[0], routes_b[0]], axis=1)
    routes = lax.all_gather(routes, "expert", axis=0, tiled=True)
    place_f = place_of(routes[:, 0], own_g, tok, cap)
    place_b = place_of(routes[:, 1], own_g, tok, cap)
    sel = lambda place: (jnp.arange(slots, dtype=jnp.int32)[:, None] == place[None, :]).astype(jnp.bfloat16)
    sel_f, sel_b = sel(place_f), sel(place_b)

    def gather(rows):
        return lax.all_gather(rows, "expert", axis=0, tiled=True, axis_index_groups=columns())

    def scatter(rows):
        return lax.psum_scatter(rows, "expert", scatter_dimension=0, tiled=True, axis_index_groups=columns())

    all_f = gather(halves(tokens, own_i))
    all_b = gather(halves(scaled, own_i))
    width = w_gate.shape[1]
    pre = jnp.dot(all_f, jnp.concatenate([w_gate, w_up], axis=1), preferred_element_type=jnp.float32)
    pre = jnp.dot(sel_f, pre.astype(jnp.bfloat16), preferred_element_type=jnp.float32)
    pre = pre + pair_swap(pre.astype(jnp.bfloat16)).astype(jnp.float32)
    hidden = (jax.nn.silu(pre[:, :width]) * pre[:, width:]).astype(jnp.bfloat16)
    hidden = contract_rows(sel_f, hidden).astype(jnp.bfloat16)
    out_f = jnp.dot(hidden, w_down, preferred_element_type=jnp.float32).astype(jnp.bfloat16)
    back_f = scatter(out_f)

    down = contract_cols(all_b, w_down)
    down = jnp.dot(sel_b, down.astype(jnp.bfloat16), preferred_element_type=jnp.float32)
    own_kept = jnp.concatenate([gate_saved[0], up_saved[0]], axis=1).astype(jnp.bfloat16)
    other = pair_swap(jnp.concatenate([down.astype(jnp.bfloat16), own_kept], axis=1)).astype(jnp.float32)
    down = down + other[:, :width]
    half = gate_saved.shape[2]

    def joined(mine, theirs):
        return jnp.where(own_i == 0, jnp.concatenate([mine, theirs], 1), jnp.concatenate([theirs, mine], 1))

    a = joined(gate_saved[0], other[:, width:width + half])
    b = joined(up_saved[0], other[:, width + half:])
    p = jax.nn.sigmoid(a)
    d_gate = (down * b * p * (1.0 + a * (1.0 - p))).astype(jnp.bfloat16)
    d_up = (down * a * p).astype(jnp.bfloat16)
    d_both = contract_rows(sel_b, jnp.concatenate([d_gate, d_up], axis=1)).astype(jnp.bfloat16)
    out_b = contract_cols(d_both, jnp.concatenate([w_gate, w_up], axis=1)).astype(jnp.bfloat16)
    back_b = scatter(out_b)

    mixed = (tokens.astype(jnp.float32) + weight_f[0] * rejoin(back_f, own_i).astype(jnp.float32)).astype(jnp.bfloat16)
    grad_in = (grads.astype(jnp.float32) + rejoin(back_b, own_i).astype(jnp.float32)).astype(jnp.bfloat16)
    return from_behind(mixed, "pipe", 1)[None], from_behind(grad_in, "pipe", 1)[None]


def solution(mesh):
    row = P("pipe", "expert", None)
    kept = P("pipe", None, "expert")
    weights = P("pipe", "expert", None, None)
    return jax.shard_map(
        per_device, mesh=mesh,
        in_specs=(row, row, row, row, row, row, kept, kept, weights, weights, weights),
        out_specs=(row, row), check_vma=False)
```

time: 779 us -> 604 us (0.78)
  waiting for transfers between devices: 640 us -> 376 us
  blocking collectives: 0 us -> 132 us
  starting transfers between devices: 99.5 us -> 54.4 us
  local copies, waits for them, and re-layouts: 18.9 us -> 4.49 us
  between operations: 1.01 us -> 14.1 us
    all_to_all x4 -> x0, waiting for transfers between devices: 630 us -> none  [the longest x1 168 us: per_device(): lax.all_to_all(spread(send_fwd, experts, capacity, splits, piece_width, s...]
    reduce_scatter x0 -> x2, waiting for transfers between devices: none -> 255 us  [scatter(): lax.psum_scatter(rows, 'expert', scatter_dimension=0, tiled=True, axis_in...]
    all_gather x0 -> x1, blocking collectives: none -> 132 us  [per_device(): routes = lax.all_gather(routes, 'expert', axis=0, tiled=True)]
    all_gather x0 -> x2, waiting for transfers between devices: none -> 109 us  [gather(): lax.all_gather(rows, 'expert', axis=0, tiled=True, axis_index_groups=colu...]
    all_to_all x4 -> x0, starting transfers between devices: 76 us -> none  [the longest x1 32.7 us: per_device(): lax.all_to_all(spread(send_fwd, experts, capacity, splits, piece_width, s...]
    ppermute x4 -> x8, starting transfers between devices: 23.5 us -> 54.3 us  [the longest x2 27.5 us: from_behind(): lax.ppermute(value, axis, [(s, (s + steps) % count) for s in range(count)])]
    reshape x4 -> x0, local copies, waits for them, and re-layouts: 12.4 us -> none  [the longest x1 4.06 us: per_device(): out_bwd.reshape(devices, capacity, piece_width)]
  transfers between devices with their start and end apart: 8 -> 12, of which waited for: 7 -> 8; matrix products, arithmetic and copies ran while one was open for 3% -> 4% of each run, Pallas kernels for 0% -> 0%
where the time goes in v1:
time: 604 us; the launch traced here: 602 us
  waiting for transfers between devices  376 us (62%)
  blocking collectives  132 us (22%)
  starting transfers between devices  54.4 us (9%)
  between operations  14.1 us (2%)
  matrix products  13.2 us (2%)
  other arithmetic  7.16 us (1%)
    reduce_scatter x2, waiting for transfers between devices, scatter(): lax.psum_scatter(rows, 'expert', scatter_dimension=0, tiled=True, axis_in...  255 us
    all_gather x1, blocking collectives, per_device(): routes = lax.all_gather(routes, 'expert', axis=0, tiled=True)  132 us
    all_gather x2, waiting for transfers between devices, gather(): lax.all_gather(rows, 'expert', axis=0, tiled=True, axis_index_groups=colu...  109 us
    ppermute x2, starting transfers between devices, from_behind(): lax.ppermute(value, axis, [(s, (s + steps) % count) for s in range(count)])  27.5 us
    ppermute x6, starting transfers between devices, pair_swap(): return lax.ppermute(value, 'expert', [(s, s ^ 1) for s in range(count)])  26.8 us
  transfers between devices with their start and end apart: 12, of which 8 were waited for; matrix products, arithmetic and copies ran while one was open for 4% of the time, Pallas kernels for 0%

profile of v1, /device:TPU:1, one launch (start us, length us, event | category | flops | bytes accessed | tf_op | source)
XLA Modules:
  0.0 601.9 jit_solution(5596571394297447016)
XLA Ops:
  7.2 1.1 fusion.11
  8.3 5.7 collective-permute-start.4
  14.0 1.6 collective-permute-done.4
  15.5 0.7 maximum_select_fusion.4
  16.3 0.9 broadcast_select_fusion.7
  17.1 4.9 collective-permute-start
  22.0 1.6 collective-permute-done
  23.6 0.7 maximum_select_fusion.2
  24.3 0.7 add_bitcast_fusion
  25.0 131.9 %all-gather = s32[64,8,2]{1,2,0:T(2,128)S(1)} all-gather(s32[1,8,2]{1,2,0:T(2,128)S(1)} %add_bitcast_fusion), channel_id=1, replica_groups=mesh['pipe'=16,'expert'=64] {'expert'}, dimensions={0}, use_global_device_ids=true | all-gather | bytes 4160 | tf_op jit(solution)/shard_map/all_gather | solution.py:75
  159.2 0.9 copy.24
  160.1 0.9 copy.25
  161.1 3.5 fusion.38
  164.8 1.9 collective-permute-start.5
  166.7 5.3 collective-permute-done.5
  172.3 3.1 convolution_convert_fusion
  175.5 108.9 %all-gather.4.cloned.1.call-done = bf16[512,3584]{1,0:T(8,128)(2,1)} async-done(((bf16[16,3584]{1,0:T(8,128)(2,1)}), bf16[512,3584]{1,0:T(8,128)(2,1)}) %all-gather.4.cloned.1.call-update) | async-done | bytes 3670032 | tf_op jit(solution)/shard_map/all_gather | solution.py:82
  284.5 3.4 fusion.37
  287.9 5.1 collective-permute-start.1
  293.0 2.3 collective-permute-done.1
  295.5 3.2 convolution_convert_fusion.1
  298.7 120.5 %reduce-scatter.5.cloned.1.call-done = bf16[16,3584]{1,0:T(8,128)(2,1)} async-done(((bf16[512,3584]{1,0:T(8,128)(2,1)}), bf16[16,3584]{1,0:T(8,128)(2,1)}) %reduce-scatter.5.cloned.1.call-update) | async-done | bytes 114704 | tf_op jit(solution)/shard_map/reduce_scatter | solution.py:85
  419.2 0.9 broadcast_select_fusion.1
  420.0 4.2 collective-permute-start.6
  424.3 134.4 %reduce-scatter.3.cloned.1.call-done = bf16[16,3584]{1,0:T(8,128)(2,1)} async-done(((bf16[512,3584]{1,0:T(8,128)(2,1)}), bf16[16,3584]{1,0:T(8,128)(2,1)}) %reduce-scatter.3.cloned.1.call-update) | async-done | bytes 114704 | tf_op jit(solution)/shard_map/reduce_scatter | solution.py:85
  558.7 0.9 broadcast_select_fusion.5
  559.6 5.0 collective-permute-start.2
  564.7 24.0 %collective-permute-start.7 = (bf16[8,7168]{1,0:T(8,128)(2,1)S(1)}, bf16[8,7168]{1,0:T(8,128)(2,1)S(1)}, u32[]{:S(2)}, u32[]{:S(2)}) collective-permute-start(bf16[8,7168]{1,0:T(8,128)(2,1)S(1)} %fusion.12), channel_id=1, source_target_pairs={{0,64},{64,128},{128,192},{192,256},{256,320},{320,384},{384,448},... | collective-permute-start | bytes 344072 | tf_op jit(solution)/shard_map/ppermute | solution.py:14
  588.8 3.4 collective-permute-start.3
  592.3 1.8 collective-permute-done.3
  594.0 0.6 copy.30
  594.7 0.6 copy.31
  (47 shorter events, 3.1 us)
Async XLA Ops:
  7.2 154.0 %copy-start = (bf16[1,1,128,3584]{3,2,1,0:T(8,128)(2,1)S(1)}, bf16[1,1,128,3584]{3,2,1,0:T(8,128)(2,1)}, u32[]{:S(2)}) copy-start(bf16[1,1,128,3584]{3,2,1,0:T(8,128)(2,1)} %param.21) | copy-start | bytes 2752516
  7.2 154.0 %all-gather.6.cloned.1.call-start = ((), (), s32[]{:S(2)}) async-start(), calls=%async_computation.4 | async-start | bytes 3784704 | tf_op jit(solution)/shard_map/all_gather | solution.py:82
  8.3 7.2 %collective-permute-start.4 = (bf16[8,3584]{1,0:T(8,128)(2,1)S(1)}, bf16[8,3584]{1,0:T(8,128)(2,1)S(1)}, u32[]{:S(2)}, u32[]{:S(2)}) collective-permute-start(bf16[8,3584]{1,0:T(8,128)(2,1)S(1)} %get-tuple-element.13), channel_id=1, source_target_pairs={{0,1},{1,0},{2,3},{3,2},{4,5},{5,4},{6,7},{7,6},{8,9},{9,8},{10,11... | collective-permute-start | bytes 172040 | tf_op jit(solution)/shard_map/ppermute | solution.py:9
  16.2 268.3 %all-gather.4.cloned.1.call-start = ((), (), s32[]{:S(2)}) async-start(), calls=%async_computation.2 | async-start | bytes 3784704 | tf_op jit(solution)/shard_map/all_gather | solution.py:82
  17.1 6.4 %collective-permute-start = (bf16[8,3584]{1,0:T(8,128)(2,1)S(1)}, bf16[8,3584]{1,0:T(8,128)(2,1)S(1)}, u32[]{:S(2)}, u32[]{:S(2)}) collective-permute-start(bf16[8,3584]{1,0:T(8,128)(2,1)S(1)} %get-tuple-element.17), channel_id=1, source_target_pairs={{0,1},{1,0},{2,3},{3,2},{4,5},{5,4},{6,7},{7,6},{8,9},{9,8},{10,11... | collective-permute-start | bytes 172040 | tf_op jit(solution)/shard_map/ppermute | solution.py:9
  24.3 394.9 %reduce-scatter.5.cloned.1.call-start = ((), (), s32[]{:S(2)}) async-start(), calls=%async_computation.5 | async-start | bytes 3784704 | tf_op jit(solution)/shard_map/reduce_scatter | solution.py:85
  161.1 11.3 %copy-start.4 = (bf16[1,1,3584,128]{3,2,1,0:T(8,128)(2,1)S(1)}, bf16[1,1,3584,128]{3,2,1,0:T(8,128)(2,1)}, u32[]{:S(2)}) copy-start(bf16[1,1,3584,128]{3,2,1,0:T(8,128)(2,1)} %param.20) | copy-start | bytes 2752516
  161.1 11.3 %copy-start.5 = (bf16[1,1,3584,128]{3,2,1,0:T(8,128)(2,1)S(1)}, bf16[1,1,3584,128]{3,2,1,0:T(8,128)(2,1)}, u32[]{:S(2)}) copy-start(bf16[1,1,3584,128]{3,2,1,0:T(8,128)(2,1)} %param.19) | copy-start | bytes 2752516
  164.8 7.2 %collective-permute-start.5 = (bf16[256,256]{1,0:T(8,128)(2,1)S(1)}, bf16[256,256]{1,0:T(8,128)(2,1)S(1)}, u32[]{:S(2)}, u32[]{:S(2)}) collective-permute-start(bf16[256,256]{1,0:T(8,128)(2,1)S(1)} %pad_maximum_fusion.5), channel_id=1, source_target_pairs={{0,1},{1,0},{2,3},{3,2},{4,5},{5,4},{6,7},{7,6},{8,9},{9,8},{10,11... | collective-permute-start | bytes 393224 | tf_op jit(solution)/shard_map/ppermute | solution.py:9
  175.5 383.2 %reduce-scatter.3.cloned.1.call-start = ((), (), s32[]{:S(2)}) async-start(), calls=%async_computation.3 | async-start | bytes 3784704 | tf_op jit(solution)/shard_map/reduce_scatter | solution.py:85
  287.9 7.5 %collective-permute-start.1 = (bf16[256,256]{1,0:T(8,128)(2,1)S(1)}, bf16[256,256]{1,0:T(8,128)(2,1)S(1)}, u32[]{:S(2)}, u32[]{:S(2)}) collective-permute-start(bf16[256,256]{1,0:T(8,128)(2,1)S(1)} %get-tuple-element.22), channel_id=1, source_target_pairs={{0,1},{1,0},{2,3},{3,2},{4,5},{5,4},{6,7},{7,6},{8,9},{9,8},{10,11... | collective-permute-start | bytes 393224 | tf_op jit(solution)/shard_map/ppermute | solution.py:9
  295.4 269.2 %copy-start.1 = (bf16[1,8,7168]{2,1,0:T(8,128)(2,1)S(1)}, bf16[1,8,7168]{2,1,0:T(8,128)(2,1)}, u32[]{:S(2)}) copy-start(bf16[1,8,7168]{2,1,0:T(8,128)(2,1)} %param.14) | copy-start | bytes 344068
  295.4 293.3 %copy-start.2 = (bf16[1,8,7168]{2,1,0:T(8,128)(2,1)S(1)}, bf16[1,8,7168]{2,1,0:T(8,128)(2,1)}, u32[]{:S(2)}) copy-start(bf16[1,8,7168]{2,1,0:T(8,128)(2,1)} %param.11) | copy-start | bytes 344068
  295.4 293.3 %copy-start.3 = (f32[1,8,1]{1,2,0:T(1,128)S(1)}, f32[1,8,1]{1,2,0:T(1,128)}, u32[]{:S(2)}) copy-start(f32[1,8,1]{1,2,0:T(1,128)} %param.13) | copy-start | bytes 100
  420.0 144.5 %collective-permute-start.6 = (bf16[8,3584]{1,0:T(8,128)(2,1)S(1)}, bf16[8,3584]{1,0:T(8,128)(2,1)S(1)}, u32[]{:S(2)}, u32[]{:S(2)}) collective-permute-start(bf16[8,3584]{1,0:T(8,128)(2,1)S(1)} %get-tuple-element.11), channel_id=1, source_target_pairs={{0,1},{1,0},{2,3},{3,2},{4,5},{5,4},{6,7},{7,6},{8,9},{9,8},{10,11... | collective-permute-start | bytes 172040 | tf_op jit(solution)/shard_map/ppermute | solution.py:9
  559.6 29.1 %collective-permute-start.2 = (bf16[8,3584]{1,0:T(8,128)(2,1)S(1)}, bf16[8,3584]{1,0:T(8,128)(2,1)S(1)}, u32[]{:S(2)}, u32[]{:S(2)}) collective-permute-start(bf16[8,3584]{1,0:T(8,128)(2,1)S(1)} %get-tuple-element.15), channel_id=1, source_target_pairs={{0,1},{1,0},{2,3},{3,2},{4,5},{5,4},{6,7},{7,6},{8,9},{9,8},{10,11... | collective-permute-start | bytes 172040 | tf_op jit(solution)/shard_map/ppermute | solution.py:9
  564.7 27.6 %collective-permute-start.7 = (bf16[8,7168]{1,0:T(8,128)(2,1)S(1)}, bf16[8,7168]{1,0:T(8,128)(2,1)S(1)}, u32[]{:S(2)}, u32[]{:S(2)}) collective-permute-start(bf16[8,7168]{1,0:T(8,128)(2,1)S(1)} %fusion.12), channel_id=1, source_target_pairs={{0,64},{64,128},{128,192},{192,256},{256,320},{320,384},{384,448},... | collective-permute-start | bytes 344072 | tf_op jit(solution)/shard_map/ppermute | solution.py:14
  588.8 5.2 collective-permute-start.3
Sparse Core Ops, SparseCore 0:
  16.3 132.8 all-gather.5
  152.4 131.9 all-gather.3
  287.9 131.2 reduce-scatter.4
  422.8 135.8 reduce-scatter.2

commit v2 on v1

v2 whole, which is shorter than its diff:
```python
import functools

import jax
import jax.numpy as jnp
from jax import lax
from jax.experimental import pallas as pl
from jax.experimental.pallas import tpu as pltpu
from jax.sharding import PartitionSpec as P

MESH = pl.DeviceIdType.MESH
F32 = jnp.float32
BF16 = jnp.bfloat16
EXT = 128
TOK = 8
CAP = 4
WORK = 15


def nt(left, right):
    return lax.dot_general(left, right, (((1,), (1,)), ((), ())), preferred_element_type=F32)


def nn(left, right):
    return lax.dot_general(left, right, (((1,), (0,)), ((), ())), preferred_element_type=F32)


def kernel(
    ndev, npipe, seg, half, piece,
    full_ref, ext_ref, kept_ref, wg_ref, wu_ref, wd_ref, out_ref,
    agf, agb, rsf, rsb, arrf, arrb, ybuf, graw, xf_send, xf_recv, xb_send, xb_recv,
    kbuf, wcat, wdv, acc, hid, dboth, atok, btok, fin, land,
    ag_send, ag_recv, rs_send, rs_recv, y_send, y_recv, p_send, p_recv, w_sem,
):
    nz = ndev // 2
    far = nz // 2
    rows = ndev * TOK
    slots = ndev * CAP
    pieces = half // piece
    sub_w = half // 2
    pipe = lax.axis_index("pipe")
    me = lax.axis_index("expert")
    own_i = lax.rem(me, 2)
    z = me // 2
    group = z // seg
    partner = me + 1 - 2 * own_i
    right = lax.rem(me + 2, ndev)
    left = lax.rem(me + ndev - 2, ndev)
    ahead = lax.rem(pipe + 1, npipe)
    behind = lax.rem(pipe + npipe - 1, npipe)
    neighbours = ((pipe, left), (pipe, right))

    def chunk_of(index):
        return lax.rem(index + 2 * nz, nz)

    copies = [
        pltpu.make_async_copy(wg_ref, wcat.at[:, pl.ds(0, 128)], w_sem.at[0]),
        pltpu.make_async_copy(wu_ref, wcat.at[:, pl.ds(128, 128)], w_sem.at[1]),
        pltpu.make_async_copy(wd_ref, wdv, w_sem.at[2]),
    ]
    for copy in copies:
        copy.start()

    barrier = pltpu.get_barrier_semaphore()
    for device in (
        (pipe, left), (pipe, right), (pipe, partner), (behind, me), (behind, partner),
    ):
        pl.semaphore_signal(barrier, inc=1, device_id=device, device_id_type=MESH)
    pl.semaphore_wait(barrier, 5)

    def to_partner(src, dst, which):
        return pltpu.make_async_remote_copy(
            src_ref=src, dst_ref=dst, send_sem=y_send.at[which], recv_sem=y_recv.at[which],
            device_id=(pipe, partner), device_id_type=MESH,
        )

    other_cols = pl.ds(pl.multiple_of((1 - own_i) * half, 128), half)
    own_cols = pl.ds(pl.multiple_of(own_i * half, 128), half)
    y_rows = to_partner(full_ref.at[:, other_cols], ybuf.at[:, pl.ds(0, half)], 0)
    y_ext = to_partner(ext_ref, ybuf.at[:, pl.ds(half, EXT)], 1)
    y_kept = to_partner(kept_ref, kbuf, 2)
    y_rows.start()
    y_ext.start()
    y_kept.start()
    y_rows.wait()
    y_ext.wait()

    def in_order(mine, theirs):
        return jnp.where(
            own_i == 0,
            jnp.concatenate([mine, theirs], axis=0),
            jnp.concatenate([theirs, mine], axis=0),
        )

    mine = full_ref[:, own_cols].astype(F32)
    theirs = ybuf[:, 0:half].astype(F32)
    my_ext = ext_ref[...].astype(F32)
    their_ext = ybuf[:, half:half + EXT].astype(F32)
    ext = in_order(my_ext[0:TOK], their_ext[0:TOK])
    w_fwd = ext[:, 32:33] + ext[:, 33:34] + ext[:, 34:35]
    w_bwd = ext[:, 35:36] + ext[:, 36:37] + ext[:, 37:38]
    agf[z, :, 0:half] = in_order(mine[0:TOK], theirs[0:TOK]).astype(BF16)
    agf[z, :, half:half + EXT] = ext.astype(BF16)
    raw = in_order(mine[TOK:], theirs[TOK:])
    graw[...] = raw.astype(BF16)
    agb[z] = (w_bwd * raw).astype(BF16)

    def ag_copy(buf, phase, chunk, way, step, sub):
        start, wide = sub * sub_w, sub_w
        if phase == 0 and sub == 1:
            wide += EXT
        ref = buf.at[chunk, :, pl.ds(start, wide)]
        return pltpu.make_async_remote_copy(
            src_ref=ref, dst_ref=ref,
            send_sem=ag_send.at[phase, way, step, sub], recv_sem=ag_recv.at[phase, chunk, sub],
            device_id=neighbours[way], device_id_type=MESH,
        )

    def ag_begin(buf, phase):
        for sub in (0, 1):
            for way in (1, 0):
                ag_copy(buf, phase, z, way, 0, sub).start()

    def ag_source(way, step):
        return chunk_of(z - step) if way == 1 else chunk_of(z + step)

    def ag_ring(buf, phase, work):
        def body(step, carry):
            for sub in (0, 1):
                for way in (1, 0):
                    copy = ag_copy(buf, phase, ag_source(way, step), way, step, sub)
                    copy.wait_recv()
                    copy.start()
            if work is not None:
                work(step)
            return carry

        lax.fori_loop(1, far - 1, body, 0)
        for sub in (0, 1):
            for way in (1, 0):
                copy = ag_copy(buf, phase, ag_source(way, far - 1), way, far - 1, sub)
                copy.wait_recv()
                if way == 1 - sub:
                    copy.start()

    def ag_end(buf, phase):
        for sub in (0, 1):
            ag_copy(buf, phase, chunk_of(z + far), 0, 0, sub).wait_recv()

    def ag_drain(buf, phase):
        def body(step, carry):
            for sub in (0, 1):
                for way in (1, 0):
                    ag_copy(buf, phase, ag_source(way, step), way, step, sub).wait_send()
            return carry

        lax.fori_loop(0, far - 1, body, 0)
        for sub in (0, 1):
            way = 1 - sub
            ag_copy(buf, phase, ag_source(way, far - 1), way, far - 1, sub).wait_send()

    def cols(index):
        return pl.ds(pl.multiple_of(index * piece, 128), piece)

    def some_pieces(first, act):
        for k in (0, 1):
            index = first + k

            @pl.when(jnp.logical_and(index >= 0, index < pieces))
            def _():
                act(index)

    f_swap = to_partner(xf_send, xf_recv, 3)
    b_swap = to_partner(xb_send, xb_recv, 4)

    def pre_piece(index):
        x = agf[:, :, cols(index)].reshape(rows, piece)
        part = nn(x, wcat[cols(index), :])

        @pl.when(index == 0)
        def _():
            acc[...] = part

        @pl.when(index > 0)
        def _():
            acc[...] += part

    def ext_all():
        return agf[:, :, half:half + EXT].reshape(rows, EXT).astype(F32)

    def place_kept():
        y_kept.wait()
        spot = ext_all()[:, 16:17] - (group * CAP).astype(F32)
        base = ((lax.broadcasted_iota(jnp.int32, (rows, slots), 0) >> 3) * CAP).astype(F32)
        lane = lax.broadcasted_iota(jnp.int32, (rows, slots), 1).astype(F32)
        within = jnp.logical_and(spot >= 0.0, spot < float(CAP))
        target = base + jnp.where(within, spot, -65536.0)
        pick = jnp.where(lane == target, 1.0, 0.0).astype(BF16)
        own = nn(pick, kept_ref[...])
        oth = nn(pick, kbuf[...])
        first = jnp.where(own_i == 0, own, oth)
        second = jnp.where(own_i == 0, oth, own)
        low = lax.broadcasted_iota(jnp.int32, (rows, 128), 1) < 64
        atok[...] = jnp.where(low, first, pltpu.roll(second, 64, 1))
        btok[...] = jnp.where(low, pltpu.roll(first, 64, 1), second)

    def activate():
        f_swap.wait()
        gate = acc[:, 0:128] + xf_recv[:, 0:128].astype(F32)
        upper = acc[:, 128:256] + xf_recv[:, 128:256].astype(F32)
        value = gate * jax.nn.sigmoid(gate) * upper
        mask = ext_all()[:, 0:1] == group.astype(F32)
        hid[...] = jnp.where(mask, value, 0.0).astype(BF16)

    def out_f_piece(index):
        part = nn(hid[...], wdv[:, cols(index)])
        rsf[:, :, cols(index)] = part.astype(BF16).reshape(nz, 16, piece)

    def f_work(step):
        some_pieces(jnp.where(step < 5, (step - 1) * 2, -2), pre_piece)

        @pl.when(step == 4)
        def _():
            xf_send[...] = acc[...].astype(BF16)
            f_swap.start()

        @pl.when(step == 5)
        def _():
            place_kept()

        @pl.when(step == 9)
        def _():
            activate()

        some_pieces(jnp.where(step >= 10, (step - 10) * 2, -2), out_f_piece)

    def down_piece(index):
        x = agb[:, :, cols(index)].reshape(rows, piece)
        part = nt(x, wdv[:, cols(index)])

        @pl.when(index == 0)
        def _():
            acc[:, 0:128] = part

        @pl.when(index > 0)
        def _():
            acc[:, 0:128] += part

    def differentiate():
        b_swap.wait()
        down = acc[:, 0:128] + xb_recv[...].astype(F32)
        a = atok[...]
        p = jax.nn.sigmoid(a)
        dboth[:, 0:128] = (down * btok[...] * p * (1.0 + a * (1.0 - p))).astype(BF16)
        dboth[:, 128:256] = (down * a * p).astype(BF16)

    def out_b_piece(index):
        part = nt(dboth[...], wcat[cols(index), :])
        rsb[:, :, cols(index)] = part.astype(BF16).reshape(nz, 16, piece)

    def b_work(step):
        some_pieces(jnp.where(step < 5, (step - 1) * 2, -2), down_piece)

        @pl.when(step == 4)
        def _():
            xb_send[...] = acc[:, 0:128].astype(BF16)
            b_swap.start()

        @pl.when(step == 8)
        def _():
            differentiate()

        some_pieces(jnp.where(step >= 9, (step - 9) * 2, -2), out_b_piece)

    def leftover(first, work):
        def body(step, carry):
            work(step)
            return carry

        lax.fori_loop(first, WORK, body, 0)

    def rs_dest(way, step):
        return chunk_of(z + far - step) if way == 1 else chunk_of(z - far + step)

    def rs_copy(buf, arr, phase, way, step, sub):
        span = pl.ds(sub * sub_w, sub_w)
        return pltpu.make_async_remote_copy(
            src_ref=buf.at[rs_dest(way, step), :, span], dst_ref=arr.at[way, step, :, span],
            send_sem=rs_send.at[phase, way, step, sub], recv_sem=rs_recv.at[phase, way, step, sub],
            device_id=neighbours[way], device_id_type=MESH,
        )

    def rs_hop(buf, arr, phase, way, step, sub, add):
        if add:
            rs_copy(buf, arr, phase, way, step - 1, sub).wait_recv()
            span = pl.ds(sub * sub_w, sub_w)
            dest = rs_dest(way, step)
            total = buf[dest, :, span].astype(F32) + arr[way, step - 1, :, span].astype(F32)
            buf[dest, :, span] = total.astype(BF16)
        rs_copy(buf, arr, phase, way, step, sub).start()

    def rs_ring(buf, arr, phase, work):
        for sub in (0, 1):
            rs_hop(buf, arr, phase, 1 - sub, 0, sub, False)
        for sub in (0, 1):
            rs_hop(buf, arr, phase, sub, 1, sub, False)
        for sub in (0, 1):
            rs_hop(buf, arr, phase, 1 - sub, 1, sub, True)
        if work is not None:
            work(1)

        def body(step, carry):
            for sub in (0, 1):
                for way in (1, 0):
                    rs_hop(buf, arr, phase, way, step, sub, True)
            if work is not None:
                work(step)
            return carry

        lax.fori_loop(2, far, body, 0)

    def rs_total(buf, arr, phase):
        for way in (1, 0):
            for sub in (0, 1):
                rs_copy(buf, arr, phase, way, far - 1, sub).wait_recv()
        return (
            buf[z].astype(F32) + arr[1, far - 1].astype(F32) + arr[0, far - 1].astype(F32)
        )

    def rs_drain(buf, arr, phase):
        for sub in (0, 1):
            rs_copy(buf, arr, phase, 1 - sub, 0, sub).wait_send()

        def body(step, carry):
            for sub in (0, 1):
                for way in (1, 0):
                    rs_copy(buf, arr, phase, way, step, sub).wait_send()
            return carry

        lax.fori_loop(1, far, body, 0)

    ag_begin(agf, 0)
    for copy in copies:
        copy.wait()
    ag_ring(agf, 0, None)
    ag_begin(agb, 1)
    ag_end(agf, 0)
    ag_ring(agb, 1, f_work)
    leftover(far - 1, f_work)
    ag_end(agb, 1)
    rs_ring(rsf, arrf, 0, b_work)
    leftover(far, b_work)
    ag_drain(agf, 0)
    ag_drain(agb, 1)
    rs_ring(rsb, arrb, 1, None)
    mixed = agf[z, :, 0:half].astype(F32) + w_fwd * rs_total(rsf, arrf, 0)
    grad = graw[...].astype(F32) + rs_total(rsb, arrb, 1)
    for y in (0, 1):
        fin[y] = jnp.concatenate(
            [mixed[y * TOK:(y + 1) * TOK], grad[y * TOK:(y + 1) * TOK]], axis=0
        ).astype(BF16)
    hand = [
        pltpu.make_async_remote_copy(
            src_ref=fin.at[y], dst_ref=land.at[own_i],
            send_sem=p_send.at[y], recv_sem=p_recv.at[own_i],
            device_id=(ahead, z * 2 + y), device_id_type=MESH,
        )
        for y in (0, 1)
    ]
    for copy in hand:
        copy.start()
    rs_drain(rsf, arrf, 0)
    rs_drain(rsb, arrb, 1)
    for copy in hand:
        copy.wait_send()
    for y in (0, 1):
        pltpu.make_async_remote_copy(
            src_ref=fin.at[y], dst_ref=land.at[y],
            send_sem=p_send.at[y], recv_sem=p_recv.at[y],
            device_id=(ahead, me), device_id_type=MESH,
        ).wait_recv()
    out_ref[...] = land[...]


def per_device(npipe, ndev, tokens, routes_f, weight_f, grads, routes_b, weight_b,
               gate_saved, up_saved, gate_proj, up_proj, down_proj):
    half = down_proj.shape[3]
    slots = gate_saved.shape[1]
    rows = ndev * TOK
    nz = ndev // 2
    experts = ndev // min(16, ndev // 2)
    seg = nz // experts
    far = nz // 2
    piece = 512 if half % 512 == 0 else 256

    full = jnp.concatenate([tokens[0], grads[0]], axis=0)
    named = routes_b[0, :, 0]
    order = jnp.arange(TOK, dtype=jnp.int32)
    earlier = jnp.logical_and(named[:, None] == named[None, :], order[None, :] < order[:, None])
    place = named * CAP + jnp.sum(earlier.astype(jnp.int32), axis=1)

    def parts(weight):
        high = lax.reduce_precision(weight, 8, 7)
        middle = lax.reduce_precision(weight - high, 8, 7)
        return [high, middle, weight - high - middle]

    ext = jnp.concatenate(
        [jnp.broadcast_to(routes_f[0].astype(F32), (TOK, 16)),
         jnp.broadcast_to(place[:, None].astype(F32), (TOK, 16))]
        + parts(weight_f[0]) + parts(weight_b[0])
        + [jnp.zeros((TOK, EXT - 38), F32)], axis=1,
    ).astype(BF16)
    ext = jnp.concatenate([ext, ext], axis=0)
    kept = jnp.concatenate([gate_saved[0], up_saved[0]], axis=1).astype(BF16)

    vmem = pl.BlockSpec(memory_space=pltpu.VMEM)
    hbm = pl.BlockSpec(memory_space=pl.ANY)
    V = pltpu.VMEM
    dma = pltpu.SemaphoreType.DMA
    landed = pl.pallas_call(
        functools.partial(kernel, ndev, npipe, seg, half, piece),
        out_shape=jax.ShapeDtypeStruct((2, 16, half), BF16),
        in_specs=[vmem, vmem, vmem, hbm, hbm, hbm],
        out_specs=vmem,
        scratch_shapes=[
            V((nz, 16, half + EXT), BF16),
            V((nz, 16, half), BF16),
            V((nz, 16, half), BF16),
            V((nz, 16, half), BF16),
            V((2, far, 16, half), BF16),
            V((2, far, 16, half), BF16),
            V((16, half + EXT), BF16),
            V((16, half), BF16),
            V((rows, 256), BF16),
            V((rows, 256), BF16),
            V((rows, 128), BF16),
            V((rows, 128), BF16),
            V((slots, 128), BF16),
            V((half, 256), BF16),
            V((128, half), BF16),
            V((rows, 256), F32),
            V((rows, 128), BF16),
            V((rows, 256), BF16),
            V((rows, 128), F32),
            V((rows, 128), F32),
            V((2, 16, half), BF16),
            V((2, 16, half), BF16),
            dma((2, 2, far, 2)),
            dma((2, nz, 2)),
            dma((2, 2, far, 2)),
            dma((2, 2, far, 2)),
            dma((5,)),
            dma((5,)),
            dma((2,)),
            dma((2,)),
            dma((3,)),
        ],
        compiler_params=pltpu.CompilerParams(
            collective_id=0, has_side_effects=True, vmem_limit_bytes=52 * 1024 * 1024
        ),
    )(full, ext, kept, gate_proj[0, 0], up_proj[0, 0], down_proj[0, 0])
    mixed = jnp.concatenate([landed[0, :TOK], landed[1, :TOK]], axis=1)
    grad_in = jnp.concatenate([landed[0, TOK:], landed[1, TOK:]], axis=1)
    return mixed[None], grad_in[None]


def solution(mesh):
    row = P("pipe", "expert", None)
    kept = P("pipe", None, "expert")
    weights = P("pipe", "expert", None, None)
    return jax.shard_map(
        functools.partial(per_device, mesh.shape["pipe"], mesh.shape["expert"]), mesh=mesh,
        in_specs=(row, row, row, row, row, row, kept, kept, weights, weights, weights),
        out_specs=(row, row), check_vma=False,
    )
```

time: 604 us -> 279 us (0.46)
  waiting for transfers between devices: 376 us -> 0 us
  Pallas kernels: 0 us -> 270 us
  blocking collectives: 132 us -> 0 us
  starting transfers between devices: 54.4 us -> 0 us
  between operations: 14.1 us -> 0.7 us
  matrix products: 13.2 us -> 0 us
    pallas_call x0 -> x1, Pallas kernels: none -> 270 us  [per_device(): pl.pallas_call(functools.partial(kernel, ndev, npipe, seg, half, piece),...]
    reduce_scatter x2 -> x0, waiting for transfers between devices: 255 us -> none  [scatter(): lax.psum_scatter(rows, 'expert', scatter_dimension=0, tiled=True, axis_in...]
    all_gather x1 -> x0, blocking collectives: 132 us -> none  [per_device(): routes = lax.all_gather(routes, 'expert', axis=0, tiled=True)]
    all_gather x2 -> x0, waiting for transfers between devices: 109 us -> none  [gather(): lax.all_gather(rows, 'expert', axis=0, tiled=True, axis_index_groups=colu...]
    ppermute x8 -> x0, starting transfers between devices: 54.3 us -> none  [the longest x2 27.5 us: from_behind(): lax.ppermute(value, axis, [(s, (s + steps) % count) for s in range(count)])]
    dot_general x4 -> x0, matrix products: 13.2 us -> none  [the longest x1 3.51 us: per_device(): jnp.dot(sel_b, down.astype(jnp.bfloat16), preferred_element_type=jnp.floa...]
    ppermute x8 -> x0, waiting for transfers between devices: 12.5 us -> none  [the longest x6 10.8 us: pair_swap(): return lax.ppermute(value, 'expert', [(s, s ^ 1) for s in range(count)])]
  transfers between devices with their start and end apart: 12 -> 0, of which waited for: 8 -> 0; matrix products, arithmetic and copies ran while one was open for 4% -> 0% of each run, Pallas kernels for 0% -> 0%
where the time goes in v2:
time: 279 us
  Pallas kernels  270 us (97%)
  other arithmetic  4.7 us (2%)
  local copies, waits for them, and re-layouts  3.64 us (1%)
    pallas_call x1, Pallas kernels, per_device(): pl.pallas_call(functools.partial(kernel, ndev, npipe, seg, half, piece),...  270 us

profile of v2, /device:TPU:1, one launch (start us, length us, event | category | flops | bytes accessed | tf_op | source)
XLA Modules:
  0.0 278.6 jit_solution(10092782745179083909)
XLA Ops:
  0.6 0.0 copy-start
  0.6 0.7 convert_bitcast_fusion.2
  1.4 0.9 convert_reduce_fusion
  2.3 0.7 convert_convert_fusion
  3.0 0.1 broadcast_in_dim.11
  3.0 0.1 broadcast_in_dim.10
  3.1 0.7 copy.19
  3.8 0.7 copy.21
  4.6 0.1 concatenate.21
  4.7 1.0 copy.23
  5.6 1.0 copy.24
  6.6 0.1 pad_maximum_fusion.1.kept_ref
  6.7 1.0 pad_maximum_fusion.full_ref
  7.7 0.0 copy-done
  7.7 269.5 %shard_map.122 = bf16[2,16,3584]{2,1,0:T(8,128)(2,1)S(1)} custom-call(bf16[16,7168]{1,0:T(8,128)(2,1)S(1)} %pad_maximum_fusion.full_ref, bf16[16,128]{1,0:T(8,128)(2,1)S(1)} %pad_maximum_fusion.2.ext_ref, bf16[256,128]{1,0:T(8,128)(2,1)S(1)} %pad_maximum_fusion.1.kept_ref, bf16[3584,128]{1,0:T(8,128)(2,1)S(1)} %bitcast.29, bf16[3584,128]{1,0:T(8,128)(2,1)} %bitcast.30, ...), custom_call_target="tpu_custom_call" | custom-call | tf_op jit(solution)/shard_map/pallas_call | solution.py:419
  277.3 0.7 maximum_bitcast_fusion.1
  277.9 0.7 maximum_bitcast_fusion
  (4 shorter events, 0.0 us)
Async XLA Ops:
  0.6 7.1 %copy-start = (bf16[1,1,3584,128]{3,2,1,0:T(8,128)(2,1)S(1)}, bf16[1,1,3584,128]{3,2,1,0:T(8,128)(2,1)}, u32[]{:S(2)}) copy-start(bf16[1,1,3584,128]{3,2,1,0:T(8,128)(2,1)} %param.19) | copy-start | bytes 2752516

commit v3 on v2

v3 whole, which is shorter than its diff:
```python
import functools

import jax
import jax.numpy as jnp
from jax import lax
from jax.experimental import pallas as pl
from jax.experimental.pallas import tpu as pltpu
from jax.sharding import PartitionSpec as P

MESH = pl.DeviceIdType.MESH
F32 = jnp.float32
BF16 = jnp.bfloat16
EXT = 128
TOK = 8
CAP = 4
SUBS = 4
LAG = 2


def nt(left, right):
    return lax.dot_general(left, right, (((1,), (1,)), ((), ())), preferred_element_type=F32)


def nn(left, right):
    return lax.dot_general(left, right, (((1,), (0,)), ((), ())), preferred_element_type=F32)


def kernel(
    ndev, npipe, seg, half, piece,
    tok_ref, grd_ref, rf_ref, wf_ref, rb_ref, wb_ref, gk_ref, uk_ref, wg_ref, wu_ref, wd_ref,
    outf_ref, outb_ref,
    agf, agb, rsf, rsb, arrf, arrb, ysf, yrf, ysb, yrb, graw, xf_send, xf_recv, xb_send, xb_recv,
    ksend, kbuf, wcat, wdv, acc, acc_b, hid, dboth, atok, btok, finf, finb, landf, landb,
    ag_send, ag_recv, rs_send, rs_recv, y_send, y_recv, x_send, x_recv, p_send, p_recv, w_sem,
):
    nz = ndev // 2
    far = nz // 2
    lag = min(LAG, far // 4)
    rows = ndev * TOK
    slots = ndev * CAP
    pieces = half // piece
    sub_w = half // SUBS
    quarter = half // 2
    pipe = lax.axis_index("pipe")
    me = lax.axis_index("expert")
    own_i = lax.rem(me, 2)
    z = me // 2
    group = z // seg
    partner = me + 1 - 2 * own_i
    right = lax.rem(me + 2, ndev)
    left = lax.rem(me + ndev - 2, ndev)
    ahead = lax.rem(pipe + 1, npipe)
    behind = lax.rem(pipe + npipe - 1, npipe)
    neighbours = ((pipe, left), (pipe, right))

    def chunk_of(index):
        return lax.rem(index + 2 * nz, nz)

    copies = [
        pltpu.make_async_copy(wg_ref, wcat.at[:, pl.ds(0, 128)], w_sem.at[0]),
        pltpu.make_async_copy(wu_ref, wcat.at[:, pl.ds(128, 128)], w_sem.at[1]),
        pltpu.make_async_copy(wd_ref, wdv, w_sem.at[2]),
    ]
    for copy in copies:
        copy.start()

    barrier = pltpu.get_barrier_semaphore()
    for device in (
        (pipe, left), (pipe, right), (pipe, partner), (behind, me), (behind, partner),
    ):
        pl.semaphore_signal(barrier, inc=1, device_id=device, device_id_type=MESH)

    other_cols = pl.ds(pl.multiple_of((1 - own_i) * half, 128), half)
    own_cols = pl.ds(pl.multiple_of(own_i * half, 128), half)

    def fold(value):
        return jnp.concatenate([value[:, 0:quarter], value[:, quarter:half]], axis=0)

    def unfold(value):
        return jnp.concatenate([value[0:TOK, 0:quarter], value[TOK:16, 0:quarter]], axis=1)

    row8 = lax.broadcasted_iota(jnp.int32, (TOK, TOK), 0)
    col8 = lax.broadcasted_iota(jnp.int32, (TOK, TOK), 1)

    def as_column(row):
        spread = jnp.broadcast_to(row, (TOK, TOK))
        return jnp.sum(jnp.where(row8 == col8, spread, 0.0), axis=1, keepdims=True)

    named_row = rb_ref[...].astype(F32)
    named = as_column(named_row)
    same = jnp.logical_and(named == jnp.broadcast_to(named_row, (TOK, TOK)), col8 < row8)
    place = named * CAP + jnp.sum(jnp.where(same, 1.0, 0.0), axis=1, keepdims=True)
    lanes = lax.broadcasted_iota(jnp.int32, (TOK, EXT), 1)
    own_ext = jnp.where(
        lanes < 16, as_column(rf_ref[...].astype(F32)), jnp.where(lanes < 32, place, 0.0)
    )
    for first, ref in ((32, wf_ref), (35, wb_ref)):
        rest = as_column(ref[...])
        for k in range(3):
            part = rest.astype(BF16).astype(F32)
            own_ext = jnp.where(lanes == first + k, part, own_ext)
            rest = rest - part
    ysf[:, 0:quarter] = fold(tok_ref[:, other_cols].astype(F32)).astype(BF16)
    ysf[:, quarter:quarter + EXT] = jnp.concatenate([own_ext, own_ext], axis=0).astype(BF16)
    ysb[...] = fold(grd_ref[:, other_cols].astype(F32)).astype(BF16)
    ksend[0:64, :] = gk_ref[...].astype(BF16)
    ksend[64:128, :] = uk_ref[...].astype(BF16)
    pl.semaphore_wait(barrier, 5)

    def to_partner(src, dst, which):
        return pltpu.make_async_remote_copy(
            src_ref=src, dst_ref=dst, send_sem=y_send.at[which], recv_sem=y_recv.at[which],
            device_id=(pipe, partner), device_id_type=MESH,
        )

    y_fwd = to_partner(ysf, yrf, 0)
    y_bwd = to_partner(ysb, yrb, 1)
    y_kept = to_partner(ksend, kbuf, 2)
    y_fwd.start()
    y_bwd.start()

    def in_order(mine, theirs):
        return jnp.where(
            own_i == 0,
            jnp.concatenate([mine, theirs], axis=0),
            jnp.concatenate([theirs, mine], axis=0),
        )

    def ag_copy(buf, phase, chunk, way, step, sub):
        start, wide = sub * sub_w, sub_w
        if phase == 0 and sub == SUBS - 1:
            wide += EXT
        ref = buf.at[chunk, :, pl.ds(start, wide)]
        return pltpu.make_async_remote_copy(
            src_ref=ref, dst_ref=ref,
            send_sem=ag_send.at[phase, way, step, sub], recv_sem=ag_recv.at[phase, chunk, sub],
            device_id=neighbours[way], device_id_type=MESH,
        )

    def last_way(sub):
        return 1 if sub < SUBS // 2 else 0

    def ag_begin(buf, phase):
        for sub in range(SUBS):
            for way in (1, 0):
                ag_copy(buf, phase, z, way, 0, sub).start()

    def ag_source(way, step):
        return chunk_of(z - step) if way == 1 else chunk_of(z + step)

    def ag_hop(buf, phase, step, act):
        for sub in range(SUBS):
            for way in (1, 0):
                copy = ag_copy(buf, phase, ag_source(way, step), way, step, sub)
                copy.wait_recv()
                copy.start()
            act(step, sub)

    def ag_any(buf, phase, step, act):
        if step < far - 1:
            ag_hop(buf, phase, step, act)
        elif step == far - 1:
            for sub in range(SUBS):
                for way in (1, 0):
                    copy = ag_copy(buf, phase, ag_source(way, step), way, step, sub)
                    copy.wait_recv()
                    if way == last_way(sub):
                        copy.start()
                act(step, sub)
        elif step == far:
            for sub in range(SUBS):
                ag_copy(buf, phase, chunk_of(z + far), 0, 0, sub).wait_recv()
                act(step, sub)

    def ag_drain(buf, phase):
        def body(step, carry):
            for sub in range(SUBS):
                for way in (1, 0):
                    ag_copy(buf, phase, ag_source(way, step), way, step, sub).wait_send()
            return carry

        lax.fori_loop(0, far - 1, body, 0)
        for sub in range(SUBS):
            way = last_way(sub)
            ag_copy(buf, phase, ag_source(way, far - 1), way, far - 1, sub).wait_send()

    def cols(index):
        return pl.ds(pl.multiple_of(index * piece, 128), piece)

    def all_pieces(act):
        def body(index, carry):
            act(index)
            return carry

        lax.fori_loop(0, pieces, body, 0)

    def rows_of(buf, step, sub):
        first = chunk_of(z - step)
        second = chunk_of(z + step)
        if isinstance(step, int) and step == far:
            second = z
        span = pl.ds(sub * sub_w, sub_w)
        return first, second, jnp.concatenate([buf[first, :, span], buf[second, :, span]], axis=0)

    def gather_into(total, first, second, part, sub):
        if sub == 0:
            total[first] = part[0:16]
            total[second] = part[16:32]
        else:
            total[first] += part[0:16]
            total[second] += part[16:32]

    def swap(phase, chunk):
        src, dst = (xf_send, xf_recv) if phase == 0 else (xb_send, xb_recv)
        return pltpu.make_async_remote_copy(
            src_ref=src.at[chunk], dst_ref=dst.at[chunk],
            send_sem=x_send.at[phase, chunk], recv_sem=x_recv.at[phase, chunk],
            device_id=(pipe, partner), device_id_type=MESH,
        )

    def swap_rows(phase, chunks):
        src, dst = (acc, xf_send) if phase == 0 else (acc_b, xb_send)
        for chunk in chunks:
            dst[chunk] = src[chunk].astype(BF16)
            swap(phase, chunk).start()

    def swap_wait(phase):
        def body(chunk, carry):
            swap(phase, chunk).wait()
            return carry

        lax.fori_loop(0, nz, body, 0)

    def pre_rows(step, sub):
        first, second, x = rows_of(agf, step, sub)
        part = nn(x, wcat[sub * sub_w:(sub + 1) * sub_w, :])
        gather_into(acc, first, second, part, sub)
        if sub == SUBS - 1:
            swap_rows(0, (first, second))

    def down_rows(step, sub):
        first, second, x = rows_of(agb, step, sub)
        part = nt(x, wdv[:, sub * sub_w:(sub + 1) * sub_w])
        gather_into(acc_b, first, second, part, sub)
        if sub == SUBS - 1:
            swap_rows(1, (first, second))

    def ext_all():
        return agf[:, :, half:half + EXT].reshape(rows, EXT).astype(F32)

    def place_kept():
        y_kept.wait()
        spot = ext_all()[:, 16:17] - (group * CAP).astype(F32)
        base = ((lax.broadcasted_iota(jnp.int32, (rows, slots), 0) >> 3) * CAP).astype(F32)
        lane = lax.broadcasted_iota(jnp.int32, (rows, slots), 1).astype(F32)
        within = jnp.logical_and(spot >= 0.0, spot < float(CAP))
        target = base + jnp.where(within, spot, -65536.0)
        pick = jnp.where(lane == target, 1.0, 0.0).astype(BF16)
        own = nt(pick, ksend[...])
        oth = nt(pick, kbuf[...])
        first = jnp.where(own_i == 0, own, oth)
        second = jnp.where(own_i == 0, oth, own)
        low = lax.broadcasted_iota(jnp.int32, (rows, 128), 1) < 64
        atok[...] = jnp.where(low, first, pltpu.roll(second, 64, 1))
        btok[...] = jnp.where(low, pltpu.roll(first, 64, 1), second)

    def activate():
        swap_wait(0)
        both = (acc[...] + xf_recv[...].astype(F32)).reshape(rows, 256)
        gate = both[:, 0:128]
        upper = both[:, 128:256]
        value = gate * jax.nn.sigmoid(gate) * upper
        mask = ext_all()[:, 0:1] == group.astype(F32)
        hid[...] = jnp.where(mask, value, 0.0).astype(BF16)

    def out_f_piece(index):
        part = nn(hid[...], wdv[:, cols(index)])
        rsf[:, :, cols(index)] = part.astype(BF16).reshape(nz, 16, piece)

    def differentiate():
        swap_wait(1)
        down = (acc_b[...] + xb_recv[...].astype(F32)).reshape(rows, 128)
        a = atok[...]
        p = jax.nn.sigmoid(a)
        dboth[:, 0:128] = (down * btok[...] * p * (1.0 + a * (1.0 - p))).astype(BF16)
        dboth[:, 128:256] = (down * a * p).astype(BF16)

    def out_b_piece(index):
        part = nt(dboth[...], wcat[cols(index), :])
        rsb[:, :, cols(index)] = part.astype(BF16).reshape(nz, 16, piece)

    def rs_dest(way, step):
        return chunk_of(z + far - step) if way == 1 else chunk_of(z - far + step)

    def rs_copy(buf, arr, phase, way, step, sub):
        span = pl.ds(sub * sub_w, sub_w)
        return pltpu.make_async_remote_copy(
            src_ref=buf.at[rs_dest(way, step), :, span], dst_ref=arr.at[way, step, :, span],
            send_sem=rs_send.at[phase, way, step, sub], recv_sem=rs_recv.at[phase, way, step, sub],
            device_id=neighbours[way], device_id_type=MESH,
        )

    def rs_hop(buf, arr, phase, way, step, sub, add):
        if add:
            rs_copy(buf, arr, phase, way, step - 1, sub).wait_recv()
            span = pl.ds(sub * sub_w, sub_w)
            dest = rs_dest(way, step)
            total = buf[dest, :, span].astype(F32) + arr[way, step - 1, :, span].astype(F32)
            buf[dest, :, span] = total.astype(BF16)
        rs_copy(buf, arr, phase, way, step, sub).start()

    def rs_step(buf, arr, phase, step):
        order = [(sub, way) for sub in range(SUBS) for way in (1, 0)]
        if isinstance(step, int) and step < 2:
            late = [(sub, way) for sub, way in order if way != last_way(sub)]
            early = [(sub, way) for sub, way in order if way == last_way(sub)]
            if step == 1:
                for sub, way in late:
                    rs_hop(buf, arr, phase, way, step, sub, False)
            for sub, way in early:
                rs_hop(buf, arr, phase, way, step, sub, step == 1)
        else:
            for sub, way in order:
                rs_hop(buf, arr, phase, way, step, sub, True)

    def rs_total(buf, arr, phase):
        for way in (1, 0):
            for sub in range(SUBS):
                rs_copy(buf, arr, phase, way, far - 1, sub).wait_recv()
        return (
            buf[z].astype(F32) + arr[1, far - 1].astype(F32) + arr[0, far - 1].astype(F32)
        )

    def rs_drain(buf, arr, phase):
        for sub in range(SUBS):
            rs_copy(buf, arr, phase, last_way(sub), 0, sub).wait_send()

        def body(step, carry):
            for sub in range(SUBS):
                for way in (1, 0):
                    rs_copy(buf, arr, phase, way, step, sub).wait_send()
            return carry

        lax.fori_loop(1, far, body, 0)

    def loop(first, last, act):
        def body(step, carry):
            act(step)
            return carry

        lax.fori_loop(first, last, body, 0)

    y_fwd.wait()
    theirs = yrf[...].astype(F32)
    ext = in_order(own_ext, theirs[0:TOK, quarter:quarter + EXT])
    agf[z, :, 0:half] = in_order(tok_ref[:, own_cols].astype(F32), unfold(theirs)).astype(BF16)
    agf[z, :, half:half + EXT] = ext.astype(BF16)
    ag_begin(agf, 0)
    w_fwd = ext[:, 32:33] + ext[:, 33:34] + ext[:, 34:35]
    w_bwd = ext[:, 35:36] + ext[:, 36:37] + ext[:, 37:38]
    y_bwd.wait()
    y_kept.start()
    raw = in_order(grd_ref[:, own_cols].astype(F32), unfold(yrb[...].astype(F32)))
    graw[...] = raw.astype(BF16)
    agb[z] = (w_bwd * raw).astype(BF16)
    for copy in copies:
        copy.wait()
    loop(1, lag + 1, lambda step: ag_hop(agf, 0, step, pre_rows))
    ag_begin(agb, 1)

    def both_gather(step):
        ag_hop(agf, 0, step, pre_rows)
        ag_hop(agb, 1, step - lag, down_rows)

    loop(lag + 1, far - 1, both_gather)
    ag_any(agf, 0, far - 1, pre_rows)
    ag_any(agb, 1, far - 1 - lag, down_rows)
    ag_any(agf, 0, far, pre_rows)
    tasks = [place_kept, activate, lambda: all_pieces(out_f_piece)]
    for step in range(far - lag, far):
        ag_any(agb, 1, step, down_rows)
        if tasks:
            tasks.pop(0)()
    while tasks:
        tasks.pop(0)()
    rs_step(rsf, arrf, 0, 0)
    ag_any(agb, 1, far, down_rows)
    tasks = [differentiate, lambda: all_pieces(out_b_piece)]
    for step in range(1, lag):
        rs_step(rsf, arrf, 0, step)
        if tasks:
            tasks.pop(0)()
    while tasks:
        tasks.pop(0)()
    for step in (lag, lag + 1):
        rs_step(rsf, arrf, 0, step)
        rs_step(rsb, arrb, 1, step - lag)

    def both_reduce(step):
        rs_step(rsf, arrf, 0, step)
        rs_step(rsb, arrb, 1, step - lag)

    loop(lag + 2, far, both_reduce)
    def hand(phase, fin, land, y, slot):
        return pltpu.make_async_remote_copy(
            src_ref=fin.at[y], dst_ref=land.at[slot],
            send_sem=p_send.at[phase, y], recv_sem=p_recv.at[phase, slot],
            device_id=(ahead, z * 2 + y), device_id_type=MESH,
        )

    def give(phase, fin, land, value):
        for y in (0, 1):
            fin[y] = fold(value[y * TOK:(y + 1) * TOK]).astype(BF16)
            hand(phase, fin, land, y, own_i).start()

    def take(phase, fin, land, out):
        for y in (0, 1):
            hand(phase, fin, land, y, y).wait_recv()
            hand(phase, fin, land, y, own_i).wait_send()
            out[:, y * half:(y + 1) * half] = unfold(land[y].astype(F32)).astype(BF16)

    rs_step(rsb, arrb, 1, far - lag)
    give(0, finf, landf, agf[z, :, 0:half].astype(F32) + w_fwd * rs_total(rsf, arrf, 0))
    loop(far - lag + 1, far, lambda step: rs_step(rsb, arrb, 1, step))
    ag_drain(agf, 0)
    ag_drain(agb, 1)
    rs_drain(rsf, arrf, 0)
    take(0, finf, landf, outf_ref)
    give(1, finb, landb, graw[...].astype(F32) + rs_total(rsb, arrb, 1))
    rs_drain(rsb, arrb, 1)
    take(1, finb, landb, outb_ref)


def per_device(npipe, ndev, tokens, routes_f, weight_f, grads, routes_b, weight_b,
               gate_saved, up_saved, gate_proj, up_proj, down_proj):
    half = down_proj.shape[3]
    slots = gate_saved.shape[1]
    rows = ndev * TOK
    nz = ndev // 2
    experts = ndev // min(16, ndev // 2)
    seg = nz // experts
    far = nz // 2
    piece = 512 if half % 512 == 0 else 256

    def flat(value):
        return value[0].reshape(1, TOK)

    kept_gate, kept_up = gate_saved[0].T, up_saved[0].T
    vmem = pl.BlockSpec(memory_space=pltpu.VMEM)
    hbm = pl.BlockSpec(memory_space=pl.ANY)
    V = pltpu.VMEM
    dma = pltpu.SemaphoreType.DMA
    outs = pl.pallas_call(
        functools.partial(kernel, ndev, npipe, seg, half, piece),
        out_shape=[jax.ShapeDtypeStruct((TOK, 2 * half), BF16)] * 2,
        in_specs=[vmem] * 8 + [hbm] * 3,
        out_specs=[vmem] * 2,
        scratch_shapes=[
            V((nz, 16, half + EXT), BF16),
            V((nz, 16, half), BF16),
            V((nz, 16, half), BF16),
            V((nz, 16, half), BF16),
            V((2, far, 16, half), BF16),
            V((2, far, 16, half), BF16),
            V((16, half // 2 + EXT), BF16),
            V((16, half // 2 + EXT), BF16),
            V((16, half // 2), BF16),
            V((16, half // 2), BF16),
            V((16, half), BF16),
            V((nz, 16, 256), BF16),
            V((nz, 16, 256), BF16),
            V((nz, 16, 128), BF16),
            V((nz, 16, 128), BF16),
            V((128, slots), BF16),
            V((128, slots), BF16),
            V((half, 256), BF16),
            V((128, half), BF16),
            V((nz, 16, 256), F32),
            V((nz, 16, 128), F32),
            V((rows, 128), BF16),
            V((rows, 256), BF16),
            V((rows, 128), F32),
            V((rows, 128), F32),
            V((2, 16, half // 2), BF16),
            V((2, 16, half // 2), BF16),
            V((2, 16, half // 2), BF16),
            V((2, 16, half // 2), BF16),
            dma((2, 2, far, SUBS)),
            dma((2, nz, SUBS)),
            dma((2, 2, far, SUBS)),
            dma((2, 2, far, SUBS)),
            dma((3,)),
            dma((3,)),
            dma((2, nz)),
            dma((2, nz)),
            dma((2, 2)),
            dma((2, 2)),
            dma((3,)),
        ],
        compiler_params=pltpu.CompilerParams(
            collective_id=0, has_side_effects=True, vmem_limit_bytes=52 * 1024 * 1024
        ),
    )(
        tokens[0], grads[0], flat(routes_f), flat(weight_f), flat(routes_b), flat(weight_b),
        kept_gate, kept_up, gate_proj[0, 0], up_proj[0, 0], down_proj[0, 0],
    )
    return outs[0][None], outs[1][None]


def solution(mesh):
    row = P("pipe", "expert", None)
    kept = P("pipe", None, "expert")
    weights = P("pipe", "expert", None, None)
    return jax.shard_map(
        functools.partial(per_device, mesh.shape["pipe"], mesh.shape["expert"]), mesh=mesh,
        in_specs=(row, row, row, row, row, row, kept, kept, weights, weights, weights),
        out_specs=(row, row), check_vma=False,
    )
```

time: 279 us -> 214 us (0.77)
  Pallas kernels: 270 us -> 206 us
  other arithmetic: 4.7 us -> 0 us
  local copies, waits for them, and re-layouts: 3.64 us -> 6.62 us
    pallas_call x1, Pallas kernels: 270 us -> 206 us  [per_device(): pl.pallas_call(functools.partial(kernel, ndev, npipe, seg, half, piece),...]
    unnamed x4 -> x20, local copies, waits for them, and re-layouts: 1.91 us -> 6.62 us
where the time goes in v3:
time: 214 us; the launch traced here: 213 us
  Pallas kernels  206 us (96%)
  local copies, waits for them, and re-layouts  6.62 us (3%)
    pallas_call x1, Pallas kernels, per_device(): pl.pallas_call(functools.partial(kernel, ndev, npipe, seg, half, piece),...  206 us
    unnamed x20, local copies, waits for them, and re-layouts  6.62 us

profile of v3, /device:TPU:1, one launch (start us, length us, event | category | flops | bytes accessed | tf_op | source)
XLA Modules:
  0.0 213.3 jit_solution(6099933954250535768)
XLA Ops:
  0.6 0.0 copy-start.8
  0.6 0.0 copy-start.5
  0.7 0.0 copy-start.6
  0.7 0.0 copy-start.7
  0.7 0.6 copy-done.8
  1.3 0.0 copy-done.5
  1.3 0.0 copy-done.6
  1.3 0.0 copy-done.7
  1.3 0.0 copy-start
  1.3 1.2 copy-done
  2.5 0.0 copy-start.1
  2.5 0.9 copy-done.1
  3.4 0.0 copy-start.2
  3.4 0.9 copy-done.2
  4.3 0.0 copy-start.3
  4.3 0.8 copy-done.3
  5.2 0.0 copy-start.4
  5.2 0.8 copy-done.4
  6.0 206.0 %shard_map.122 = (bf16[8,7168]{1,0:T(8,128)(2,1)S(1)}, bf16[8,7168]{1,0:T(8,128)(2,1)S(1)}) custom-call(bf16[8,7168]{1,0:T(8,128)(2,1)S(1)} %bitcast.20, bf16[8,7168]{1,0:T(8,128)(2,1)S(1)} %bitcast.21, s32[1,8]{1,0:T(1,128)S(1)} %bitcast.24, f32[1,8]{1,0:T(1,128)S(1)} %bitcast.25, s32[1,8]{1,0:T(1,128)S(1)} %bitcast.26, f32[1,8]{1,0:T(1,128)S(1)} %bitcast.27, ...), custom_call_target="tpu_custom_call" | custom-call | tf_op jit(solution)/shard_map/pallas_call | solution.py:453
  212.0 0.6 copy.15
  212.6 0.6 copy.16
Async XLA Ops:
  0.6 0.7 copy-start.8
  0.6 0.7 copy-start.5
  0.7 0.7 copy-start.6
  0.7 0.7 copy-start.7
  1.3 1.2 copy-start
  2.5 0.9 copy-start.1
  3.4 0.9 copy-start.2
  4.3 0.8 copy-start.3
  5.2 0.8 copy-start.4

commit v4 on v3

--- a/solution.py
+++ b/solution.py
@@ -27,9 +27,9 @@
 
 def kernel(
     ndev, npipe, seg, half, piece,
-    tok_ref, grd_ref, rf_ref, wf_ref, rb_ref, wb_ref, gk_ref, uk_ref, wg_ref, wu_ref, wd_ref,
+    tok_hbm, grd_hbm, rf_ref, wf_ref, rb_ref, wb_ref, gk_hbm, uk_hbm, wg_ref, wu_ref, wd_ref,
     outf_ref, outb_ref,
-    agf, agb, rsf, rsb, arrf, arrb, ysf, yrf, ysb, yrb, graw, xf_send, xf_recv, xb_send, xb_recv,
+    tok_ref, grd_ref, gk_ref, uk_ref, agf, agb, rsf, rsb, arrf, arrb, ysf, yrf, ysb, yrb, graw, xf_send, xf_recv, xb_send, xb_recv,
     ksend, kbuf, wcat, wdv, acc, acc_b, hid, dboth, atok, btok, finf, finb, landf, landb,
     ag_send, ag_recv, rs_send, rs_recv, y_send, y_recv, x_send, x_recv, p_send, p_recv, w_sem,
 ):
@@ -56,14 +56,19 @@
     def chunk_of(index):
         return lax.rem(index + 2 * nz, nz)
 
+    early = [
+        pltpu.make_async_copy(src, dst, w_sem.at[3 + k])
+        for k, (src, dst) in enumerate(
+            ((tok_hbm, tok_ref), (grd_hbm, grd_ref), (gk_hbm, gk_ref), (uk_hbm, uk_ref))
+        )
+    ]
+    for copy in early:
+        copy.start()
     copies = [
         pltpu.make_async_copy(wg_ref, wcat.at[:, pl.ds(0, 128)], w_sem.at[0]),
         pltpu.make_async_copy(wu_ref, wcat.at[:, pl.ds(128, 128)], w_sem.at[1]),
         pltpu.make_async_copy(wd_ref, wdv, w_sem.at[2]),
     ]
-    for copy in copies:
-        copy.start()
-
     barrier = pltpu.get_barrier_semaphore()
     for device in (
         (pipe, left), (pipe, right), (pipe, partner), (behind, me), (behind, partner),
@@ -86,6 +91,8 @@
         spread = jnp.broadcast_to(row, (TOK, TOK))
         return jnp.sum(jnp.where(row8 == col8, spread, 0.0), axis=1, keepdims=True)
 
+    for copy in copies:
+        copy.start()
     named_row = rb_ref[...].astype(F32)
     named = as_column(named_row)
     same = jnp.logical_and(named == jnp.broadcast_to(named_row, (TOK, TOK)), col8 < row8)
@@ -100,11 +107,11 @@
             part = rest.astype(BF16).astype(F32)
             own_ext = jnp.where(lanes == first + k, part, own_ext)
             rest = rest - part
+    early[0].wait()
     ysf[:, 0:quarter] = fold(tok_ref[:, other_cols].astype(F32)).astype(BF16)
     ysf[:, quarter:quarter + EXT] = jnp.concatenate([own_ext, own_ext], axis=0).astype(BF16)
+    early[1].wait()
     ysb[...] = fold(grd_ref[:, other_cols].astype(F32)).astype(BF16)
-    ksend[0:64, :] = gk_ref[...].astype(BF16)
-    ksend[64:128, :] = uk_ref[...].astype(BF16)
     pl.semaphore_wait(barrier, 5)
 
     def to_partner(src, dst, which):
@@ -118,6 +125,10 @@
     y_kept = to_partner(ksend, kbuf, 2)
     y_fwd.start()
     y_bwd.start()
+    early[2].wait()
+    early[3].wait()
+    ksend[0:64, :] = gk_ref[...].astype(BF16)
+    ksend[64:128, :] = uk_ref[...].astype(BF16)
 
     def in_order(mine, theirs):
         return jnp.where(
@@ -447,15 +458,19 @@
 
     kept_gate, kept_up = gate_saved[0].T, up_saved[0].T
     vmem = pl.BlockSpec(memory_space=pltpu.VMEM)
-    hbm = pl.BlockSpec(memory_space=pl.ANY)
+    hbm = pl.BlockSpec(memory_space=pltpu.HBM)
     V = pltpu.VMEM
     dma = pltpu.SemaphoreType.DMA
     outs = pl.pallas_call(
         functools.partial(kernel, ndev, npipe, seg, half, piece),
         out_shape=[jax.ShapeDtypeStruct((TOK, 2 * half), BF16)] * 2,
-        in_specs=[vmem] * 8 + [hbm] * 3,
+        in_specs=[hbm] * 2 + [vmem] * 4 + [hbm] * 5,
         out_specs=[vmem] * 2,
         scratch_shapes=[
+            V((TOK, 2 * half), BF16),
+            V((TOK, 2 * half), BF16),
+            V((64, slots), F32),
+            V((64, slots), F32),
             V((nz, 16, half + EXT), BF16),
             V((nz, 16, half), BF16),
             V((nz, 16, half), BF16),
@@ -495,10 +510,10 @@
             dma((2, nz)),
             dma((2, 2)),
             dma((2, 2)),
-            dma((3,)),
+            dma((7,)),
         ],
         compiler_params=pltpu.CompilerParams(
-            collective_id=0, has_side_effects=True, vmem_limit_bytes=52 * 1024 * 1024
+            collective_id=0, has_side_effects=True, vmem_limit_bytes=60 * 1024 * 1024
         ),
     )(
         tokens[0], grads[0], flat(routes_f), flat(weight_f), flat(routes_b), flat(weight_b),

time: 214 us -> 210 us (0.981)
  local copies, waits for them, and re-layouts: 6.62 us -> 2.24 us
    unnamed x20 -> x4, local copies, waits for them, and re-layouts: 6.62 us -> 2.24 us
where the time goes in v4:
time: 210 us
  Pallas kernels  207 us (99%)
  local copies, waits for them, and re-layouts  2.24 us (1%)
    pallas_call x1, Pallas kernels, per_device(): pl.pallas_call(functools.partial(kernel, ndev, npipe, seg, half, piece),...  207 us

profile of v4, /device:TPU:1, one launch (start us, length us, event | category | flops | bytes accessed | tf_op | source)
XLA Modules:
  0.0 209.7 jit_solution(6800982402240005039)
XLA Ops:
  0.6 206.8 %shard_map.122 = (bf16[8,7168]{1,0:T(8,128)(2,1)}, bf16[8,7168]{1,0:T(8,128)(2,1)}) custom-call(bf16[8,7168]{1,0:T(8,128)(2,1)} %bitcast.22, bf16[8,7168]{1,0:T(8,128)(2,1)} %bitcast.23, s32[1,8]{1,0:T(1,128)} %bitcast.26, f32[1,8]{1,0:T(1,128)} %bitcast.27, s32[1,8]{1,0:T(1,128)} %bitcast.28, f32[1,8]{1,0:T(1,128)} %bitcast.29, f32[64,256]{1,0:T(8,128)} %bitcast.24, ...), custom_call_target="tpu_custom_call" | custom-call | tf_op jit(solution)/shard_map/pallas_call | solution.py:464
  207.5 0.0 copy-start
  207.5 1.6 copy.15
  209.1 0.0 copy-done
  209.1 0.6 copy.16
Async XLA Ops:
  207.5 1.6 copy-start
